TPU v7x, 32 devices: a whole 2x2x4 slice. The times are simulated.
32 devices in a mesh: dp: 8 (over z, y), feat: 4 (over x, core).
Axes of the slice: x: 2, y: 2, z: 4, core: 2. Of those that a mesh axis runs over, the one named last changes fastest.
Arguments:
- hidden_in: bfloat16 [24, 1024, 768], P('dp', 'feat'), may hold values from -6 to 6
- norm1_gain: float32 [768], replicated, may hold values from 0.5 to 1.5
- norm1_bias: float32 [768], replicated, may hold values from -1.5 to 1.5
- qkv_weight: bfloat16 [768, 2304], replicated, may hold values from -0.21875 to 0.21875
- qkv_bias: float32 [2304], replicated, may hold values from -1.5 to 1.5
- feature_draws: bfloat16 [12, 64, 256], P(None, None, 'feat'), may hold values from -2 to 2
- out_weight: bfloat16 [768, 768], replicated, may hold values from -3.5 to 3.5
- out_bias: float32 [768], replicated, may hold values from -1.5 to 1.5
- norm2_gain: float32 [768], replicated, may hold values from 0.5 to 1.5
- norm2_bias: float32 [768], replicated, may hold values from -1.5 to 1.5
- up_weight: bfloat16 [768, 3072], replicated, may hold values from -0.21875 to 0.21875
- up_bias: float32 [3072], replicated, may hold values from -1.5 to 1.5
- down_weight: bfloat16 [3072, 768], replicated, may hold values from -0.15625 to 0.15625
- down_bias: float32 [768], replicated, may hold values from -1.5 to 1.5
- block_bucket: int32 [24, 16, 1], P('dp'), may hold values from 0 to 3; in each aligned block of 16 rows (0 to 15, 16 to 31, ..., all dimensions but the last counted through in order) at most 8 rows name the same one
- out_grad: bfloat16 [24, 1024, 768], P('dp', 'feat'), may hold values from -6 to 6
Outputs:
- layer_out: bfloat16 [24, 1024, 768], P('dp', 'feat')
- input_grad: float32 [24, 1024, 768], P('dp', 'feat')
- norm1_gain_grad: float32 [768], P(('dp', 'feat'))
- norm1_bias_grad: float32 [768], P(('dp', 'feat'))
- qkv_weight_grad: float32 [768, 2304], P(('dp', 'feat'))
- qkv_bias_grad: float32 [2304], P(('dp', 'feat'))
- out_weight_grad: float32 [768, 768], P(('dp', 'feat'))
- out_bias_grad: float32 [768], P(('dp', 'feat'))
- norm2_gain_grad: float32 [768], P(('dp', 'feat'))
- norm2_bias_grad: float32 [768], P(('dp', 'feat'))
- up_weight_grad: float32 [768, 3072], P(('dp', 'feat'))
- up_bias_grad: float32 [3072], P(('dp', 'feat'))
- down_weight_grad: float32 [3072, 768], P(('dp', 'feat'))
- down_bias_grad: float32 [768], P(('dp', 'feat'))
Inputs may be any that keep to these rules, and one draw needn't show every extreme that they name: `block_bucket`: within each sequence no bucket holds more than 8 of its 16 blocks; in some sequence one bucket holds exactly 8.
All inputs are finite; a program needn't handle non-finite values.
Results may differ from a plain program's by a relative error of at most 0.024.
Values may be sent and summed in bfloat16 or wider, within the bound.
A program may use at most 384 MiB of HBM per device.

v0:
```python
import math

import jax
import jax.numpy as jnp
from jax import lax
from jax.experimental import pallas as pl
from jax.experimental.pallas import tpu as pltpu
from jax.sharding import PartitionSpec as P

HD = 64
FEAT = 256
BLOCK = 64
NBUCK = 4
GROUP = 4
CHUNK = 256
STATES = NBUCK * HD + 16
FAR = 16384.0
VMEM = 60 * 1024 * 1024

F32 = jnp.float32
BF16 = jnp.bfloat16
MESH = pl.DeviceIdType.MESH


def mat(left, right):
    return jnp.dot(left, right, preferred_element_type=F32)


def mat_nt(left, right):
    return lax.dot_general(left, right, (((1,), (1,)), ((), ())), preferred_element_type=F32)


def mat_tn(left, right):
    return lax.dot_general(left, right, (((0,), (0,)), ((), ())), preferred_element_type=F32)


def row_stats(values):
    row_mean = jnp.mean(values, axis=-1, keepdims=True)
    centered = values - row_mean
    scale = lax.rsqrt(jnp.mean(centered * centered, axis=-1, keepdims=True) + 1e-05)
    return (centered * scale, scale)


def norm_back(cotangent, normed, scale):
    mean_one = jnp.mean(cotangent, axis=-1, keepdims=True)
    mean_two = jnp.mean(cotangent * normed, axis=-1, keepdims=True)
    return scale * (cotangent - mean_one - normed * mean_two)


def features(vectors, draws):
    wide = vectors.astype(F32)
    square = jnp.sum(wide * wide, axis=0, keepdims=True) * (0.5 / math.sqrt(HD))
    return jnp.exp(mat_tn(draws, vectors) - (square + 0.5 * math.log(FEAT)))


def spread(rows, marks):
    return [rows * marks[u : u + 1] for u in range(NBUCK)]


def pick(stacked, marks):
    total = stacked[0:HD] * marks[0:1]
    for u in range(1, NBUCK):
        total = total + stacked[u * HD : (u + 1) * HD] * marks[u : u + 1]
    return total


def away_marks(hot):
    live = (lax.broadcasted_iota(jnp.int32, hot.shape, 0) < NBUCK).astype(F32)
    return live - hot.astype(F32)


def partner(own, r):
    x, core = own // 2, own % 2
    if r & 2:
        x = 1 - x
    if r & 1:
        core = 1 - core
    return 2 * x + core


def as_row(ref):
    return ref[...].reshape(1, ref.shape[0])


def aligned(count):
    return -(-count // 16) * 16


def remote(src, dst, send, recv, place):
    return pltpu.make_async_remote_copy(
        src_ref=src, dst_ref=dst, send_sem=send, recv_sem=recv, device_id=place, device_id_type=MESH
    )


def head_rows(h, kind, heads):
    return pl.ds(pl.multiple_of((kind * heads + h) * HD, HD), HD)


def attend_kernel(
    bucket, hidden, gain_ref, shift_ref, bias_ref, weight_any, draws_in, grad, down_any,
    parts_any, mix_any, act_grad_any, proj_out, state_out, mixed_out, den_out, hot_out, weight_out, draws_out,
    soft_out, phi_q_out, phi_k_out,
    parts, mix_land, mix_send, raw, bias_row, bias_scr, draws_land, down_vm, act_grad,
    query_scr, key_scr, value_scr, low_scr,
    raw_sem, part_send, part_recv, draw_send, draw_recv, mix_send_sem, mix_recv_sem, out_sem,
    down_sem, act_sem,
):
    s, h = pl.program_id(0), pl.program_id(1)
    seqs, rows, model = hidden.shape
    heads = draws_out.shape[0]
    total = GROUP * rows
    width = heads * HD
    own = lax.axis_index("feat")
    near, across = {"feat": partner(own, 1)}, {"feat": partner(own, 2)}

    def part_copy(q, kind):
        src, dst, place = ((0, 1, near), (0, 2, across), (2, 3, near))[kind]
        return remote(
            parts.at[q, src], parts.at[q, dst], part_send.at[q, kind], part_recv.at[q, kind], place
        )

    def draw_copy(r):
        other = partner(own, r)
        return remote(
            draws_in.at[pl.ds(other * heads, heads)], draws_land.at[r - 1],
            draw_send.at[r - 1], draw_recv.at[r - 1], {"feat": other},
        )

    def mix_copy(q, g, r):
        span = pl.ds(pl.multiple_of(g * HD, HD), HD)
        return remote(
            mix_send.at[q, r - 1, span], mix_land.at[q, r, span], mix_send_sem.at[q, g, r - 1],
            mix_recv_sem.at[q, g, r - 1], {"feat": partner(own, r)},
        )

    down_copy = pltpu.make_async_copy(down_any, down_vm, down_sem)
    act_copy = pltpu.make_async_copy(act_grad, act_grad_any, act_sem)

    def raw_copy(j):
        cols = pl.ds(pl.multiple_of(j * model + (own // 2) * 2 * width, 2 * width), 2 * width)
        return pltpu.make_async_copy(weight_any.at[:, cols], raw.at[j], raw_sem.at[j])

    def out_copy(q):
        return pltpu.make_async_copy(parts.at[q], parts_any.at[q], out_sem.at[q])

    @pl.when((s == 0) & (h == 0))
    def _():
        for j in range(3):
            raw_copy(j).start()
        down_copy.start()
        barrier = pltpu.get_barrier_semaphore()
        for r in (1, 2, 3):
            pl.semaphore_signal(
                barrier, inc=1, device_id={"feat": partner(own, r)}, device_id_type=MESH
            )
        gain, shift = as_row(gain_ref), as_row(shift_ref)
        first = row_stats(hidden[0].astype(F32))[0] * gain + shift
        parts[0, 0] = first.astype(BF16)
        pl.semaphore_wait(barrier, 3)
        part_copy(0, 1).start()
        part_copy(0, 0).start()
        for r in (1, 2, 3):
            draw_copy(r).start()
        for q in range(1, seqs):
            normed = row_stats(hidden[q].astype(F32))[0] * gain + shift
            parts[q, 0] = normed.astype(BF16)
            part_copy(q, 1).start()
            part_copy(q, 0).start()
        core = own % 2
        bias_row[...] = as_row(bias_ref)
        for j in range(3):
            raw_copy(j).wait()
            piece = raw[j].astype(F32)
            piece = jnp.where(core == 0, piece[:, 0:width], piece[:, width:])
            weight_out[j * width : (j + 1) * width] = piece.T.astype(BF16)
            cols = pl.ds(pl.multiple_of(j * model + (own // 2) * 2 * width, 2 * width), 2 * width)
            pair = jnp.broadcast_to(bias_row[:, cols], (128, 2 * width))
            pair = jnp.where(core == 0, pair[:, 0:width], pair[:, width:])
            bias_scr[j * width : (j + 1) * width] = pair.T
        down_copy.wait()
        for t in range(act_grad.shape[0]):
            tile = down_vm[t * model : (t + 1) * model]
            for q in range(seqs):
                act_grad[t, q * rows : (q + 1) * rows] = mat_nt(grad[q], tile).astype(BF16)
        act_copy.start()
        part_copy(0, 1).wait_recv()
        part_copy(0, 2).start()
        for r in (1, 2, 3):
            draw_copy(r).wait_recv()
        mine = draws_in[pl.ds(own * heads, heads)]
        draws_out[...] = jnp.concatenate(
            [mine] + [draws_land[r - 1] for r in (1, 2, 3)], axis=2
        )

    @pl.when(h == 0)
    def _():
        per = rows // BLOCK
        lanes = lax.broadcasted_iota(jnp.int32, (16, total), 1) // BLOCK
        level = lax.broadcasted_iota(jnp.int32, (16, total), 0)
        ids = jnp.full((16, total), -1, jnp.int32)
        for r in range(GROUP):
            for i in range(per):
                ids = jnp.where(
                    lanes == r * per + i, bucket[s, partner(own, r) * per + i, 0], ids
                )
        hot_out[...] = (ids == level).astype(F32).astype(BF16)

        def project(r):
            cols = slice(r * rows, (r + 1) * rows)
            piece = mat_nt(weight_out[...], parts[s, r]) + bias_scr[:, 0:1]
            proj_out[:, cols] = piece.astype(BF16)

        project(0)
        part_copy(s, 0).wait_recv()
        project(1)
        project(2)
        part_copy(s, 2).wait_recv()
        project(3)
        out_copy(s).start()

    query = proj_out[head_rows(h, 0, heads)]
    key = proj_out[head_rows(h, 1, heads)]
    value = proj_out[head_rows(h, 2, heads)]
    draws = draws_out[h]
    hot = hot_out[...]
    hot_wide = hot.astype(F32)
    away = away_marks(hot).astype(BF16)
    phi_q = features(query, draws).astype(BF16)
    phi_k = features(key, draws).astype(BF16)
    phi_q_out[...] = phi_q
    phi_k_out[...] = phi_k
    spread_value = jnp.concatenate(spread(value, away) + [away], axis=0)
    state = mat_nt(spread_value, phi_k).astype(BF16)
    state_out[...] = state
    low = mat(state, phi_q)
    low_scr[0:HD] = pick(low, hot_wide)
    low_den = jnp.sum(low[NBUCK * HD :] * hot_wide, axis=0, keepdims=True)
    low_scr[HD : HD + 8] = jnp.broadcast_to(low_den, (8, total))
    query_scr[...] = jnp.concatenate([query * (1.0 / math.sqrt(HD)), hot], axis=0).astype(BF16)
    key_scr[...] = jnp.concatenate([key, away * -FAR], axis=0).astype(F32).T.astype(BF16)
    value_scr[0:HD] = value
    value_scr[HD:] = jnp.ones((16, total), BF16)

    head_span = pl.ds(pl.multiple_of(h * HD, HD), HD)
    score = mat(key_scr[...], query_scr[:, 0:CHUNK])
    for c in range(total // CHUNK):
        cols = slice(c * CHUNK, (c + 1) * CHUNK)
        ahead = slice((c + 1) * CHUNK, (c + 2) * CHUNK)
        later = mat(key_scr[...], query_scr[:, ahead]) if ahead.stop <= total else None
        weights = jnp.exp(score).astype(BF16)
        score = later
        soft_out[:, cols] = weights
        exact = mat(value_scr[...], weights)
        den = low_scr[HD : HD + 8, cols] + exact[HD : HD + 8]
        mixed = (low_scr[0:HD, cols] + exact[0:HD]) / den[0:1]
        mixed_out[:, cols] = mixed
        den_out[:, cols] = den
        mixed_low = mixed.astype(BF16)
        for r in range(GROUP):
            low_col, high_col = max(cols.start, r * rows), min(cols.stop, (r + 1) * rows)
            if low_col < high_col:
                piece = mixed_low[:, low_col - cols.start : high_col - cols.start]
                inner = slice(low_col - r * rows, high_col - r * rows)
                if r:
                    mix_send[s, r - 1, head_span, inner] = piece
                else:
                    mix_land[s, 0, head_span, inner] = piece
    for r in (2, 3, 1):
        mix_copy(s, h, r).start()

    @pl.when((h == heads - 2) & (s < seqs - 1))
    def _():
        part_copy(s + 1, 1).wait_recv()
        part_copy(s + 1, 2).start()

    @pl.when((s == seqs - 1) & (h == heads - 1))
    def _():
        for q in range(seqs):
            for g in range(heads):
                for r in (1, 2, 3):
                    mix_copy(q, g, r).wait_recv()
        done = pltpu.make_async_copy(mix_land, mix_any, out_sem.at[seqs])
        done.start()
        for q in range(seqs):
            for kind in range(3):
                part_copy(q, kind).wait_send()
            for g in range(heads):
                for r in (1, 2, 3):
                    mix_copy(q, g, r).wait_send()
            out_copy(q).wait()
        act_copy.wait()
        for r in (1, 2, 3):
            draw_copy(r).wait_send()
        done.wait()


def attend(bucket, hidden, gain, shift, bias, weight, draws, grad, down):
    seqs, rows, model = hidden.shape
    tiles = down.shape[0] // model
    heads = draws.shape[0] // GROUP
    width = heads * HD
    total = GROUP * rows
    whole = lambda *shape: pl.BlockSpec(shape, lambda s, h: (0,) * len(shape))
    by_seq = lambda *shape: pl.BlockSpec((None,) + shape, lambda s, h: (s,) + (0,) * len(shape))
    by_head = lambda *shape: pl.BlockSpec(
        (None, None) + shape, lambda s, h: (s, h) + (0,) * len(shape)
    )
    anywhere = pl.BlockSpec(memory_space=pl.ANY)
    return pl.pallas_call(
        attend_kernel,
        grid=(seqs, heads),
        out_shape=(
            jax.ShapeDtypeStruct((seqs, GROUP, rows, model), BF16),
            jax.ShapeDtypeStruct((seqs, GROUP, width, rows), BF16),
            jax.ShapeDtypeStruct((tiles, seqs * rows, model), BF16),
            jax.ShapeDtypeStruct((seqs, 3 * width, total), BF16),
            jax.ShapeDtypeStruct((seqs, heads, STATES, FEAT), BF16),
            jax.ShapeDtypeStruct((seqs, heads, HD, total), F32),
            jax.ShapeDtypeStruct((seqs, heads, 8, total), F32),
            jax.ShapeDtypeStruct((seqs, 16, total), BF16),
            jax.ShapeDtypeStruct((3 * width, model), BF16),
            jax.ShapeDtypeStruct((heads, HD, FEAT), BF16),
            jax.ShapeDtypeStruct((seqs, heads, total, total), BF16),
            jax.ShapeDtypeStruct((seqs, heads, FEAT, total), BF16),
            jax.ShapeDtypeStruct((seqs, heads, FEAT, total), BF16),
        ),
        in_specs=[
            pl.BlockSpec(memory_space=pltpu.SMEM),
            whole(seqs, rows, model), whole(model), whole(model), whole(3 * model), anywhere,
            whole(*draws.shape), whole(seqs, rows, model), anywhere,
        ],
        out_specs=(
            anywhere, anywhere, anywhere, by_seq(3 * width, total), by_head(STATES, FEAT), by_head(HD, total),
            by_head(8, total), by_seq(16, total), whole(3 * width, model), whole(heads, HD, FEAT),
            by_head(total, total), by_head(FEAT, total), by_head(FEAT, total),
        ),
        scratch_shapes=[
            pltpu.VMEM((seqs, GROUP, rows, model), BF16),
            pltpu.VMEM((seqs, GROUP, width, rows), BF16),
            pltpu.VMEM((seqs, 3, width, rows), BF16),
            pltpu.VMEM((3, model, 2 * width), BF16),
            pltpu.VMEM((1, 3 * model), F32),
            pltpu.VMEM((3 * width, 128), F32),
            pltpu.VMEM((3, heads, HD, draws.shape[2]), BF16),
            pltpu.VMEM(down.shape, BF16),
            pltpu.VMEM((tiles, seqs * rows, model), BF16),
            pltpu.VMEM((HD + 16, total), BF16),
            pltpu.VMEM((total, HD + 16), BF16),
            pltpu.VMEM((HD + 16, total), BF16),
            pltpu.VMEM((HD + 8, total), F32),
            pltpu.SemaphoreType.DMA((3,)),
            pltpu.SemaphoreType.DMA((seqs, 3)),
            pltpu.SemaphoreType.DMA((seqs, 3)),
            pltpu.SemaphoreType.DMA((3,)),
            pltpu.SemaphoreType.DMA((3,)),
            pltpu.SemaphoreType.DMA((seqs, heads, 3)),
            pltpu.SemaphoreType.DMA((seqs, heads, 3)),
            pltpu.SemaphoreType.DMA((seqs + 1,)),
            pltpu.SemaphoreType.DMA,
            pltpu.SemaphoreType.DMA,
        ],
        compiler_params=pltpu.CompilerParams(
            vmem_limit_bytes=VMEM, collective_id=1, has_side_effects=True
        ),
        cost_estimate=pl.CostEstimate(
            flops=24_000_000_000, bytes_accessed=20_000_000, transcendentals=0
        ),
        name="attend",
    )(bucket, hidden, gain, shift, bias, weight, draws, grad, down)


def block_kernel(
    direct, parts_ref, hidden, grad, out_w, out_b, gain_ref, shift_ref, down_b, up_b, up, down,
    act_grad_ref,
    layer_out, resid_out, grads_any, first_any, slab_any, down_any, up_any, tail_any,
    mixed_t, resid_scr, in_scr, in_t, acc_out, acc_in, act_scr, pre_scr, vec_scr, bias_row, back_t,
    slab_vm, down_vm, up_vm, tail_vm, grads_vm, first_land, send_sem, recv_sem, out_sem,
):
    step = pl.program_id(0)
    model = hidden.shape[1]
    count = hidden.shape[0] // CHUNK
    tiles = act_scr.shape[0]
    spans = [slice(c * CHUNK, (c + 1) * CHUNK) for c in range(count)]
    owners = slab_vm.shape[0] if direct else tail_vm.shape[0]
    small = model // owners
    share = tiles * small
    own = lax.axis_index("feat")
    barrier = pltpu.get_barrier_semaphore()

    part = model // GROUP

    def group_rows(r):
        return pl.ds(pl.multiple_of(partner(own, r) * part, part), part)

    def grad_copy(r):
        return remote(
            grads_vm.at[0, r], first_land.at[r - 1], send_sem.at[r - 1], recv_sem.at[r - 1],
            {"feat": partner(own, r)},
        )

    def out_copy(i):
        pieces = [(down_vm, down_any), (up_vm, up_any), (tail_vm, tail_any)]
        if direct:
            cuts = (0, share, 2 * share, slab_vm.shape[1])
            pieces = [
                (slab_vm.at[:, pl.ds(low, high - low)], slab_any.at[:, pl.ds(low, high - low)])
                for low, high in zip(cuts, cuts[1:])
            ]
        src, dst = (
            *pieces, (grads_vm, grads_any), (first_land, first_any),
        )[i]
        return pltpu.make_async_copy(src, dst, out_sem.at[i])

    @pl.when(step == 0)
    def _():
        for r in (1, 2, 3):
            pl.semaphore_signal(
                barrier, inc=1, device_id={"feat": partner(own, r)}, device_id_type=MESH
            )
        for c, span in enumerate(spans):
            for r in range(GROUP):
                mixed_t[group_rows(r), span] = parts_ref[c, r]
            resid = hidden[span].astype(F32) + mat_tn(mixed_t[:, span], out_w[...]) + as_row(out_b)
            resid_scr[span] = resid
            normed, _ = row_stats(resid)
            inner = normed * as_row(gain_ref) + as_row(shift_ref)
            in_scr[span] = inner.astype(BF16)
            in_t[:, span] = inner.T.astype(BF16)
        acc_out[...] = jnp.zeros_like(acc_out)
        acc_in[...] = jnp.zeros_like(acc_in)
        bias_row[...] = as_row(up_b)

    slope = math.sqrt(2.0 / math.pi)
    total = jnp.zeros((1, model), F32)
    up_bias = bias_row[:, pl.ds(pl.multiple_of(step * model, model), model)]
    for span in spans:
        pre = mat(in_scr[span], up[...]) + up_bias
        square = pre * pre
        tanh = jnp.tanh(pre * (slope + (slope * 0.044715) * square))
        half = 0.5 * (1.0 + tanh)
        act = (pre * half).astype(BF16)
        bend = half + (0.5 * pre) * (1.0 - tanh * tanh) * (
            slope + (3.0 * slope * 0.044715) * square
        )
        pre_grad = act_grad_ref[span].astype(F32) * bend
        total = total + jnp.sum(pre_grad, axis=0, keepdims=True)
        pre_low = pre_grad.astype(BF16)
        act_scr[step, span] = act
        pre_scr[step, span] = pre_low
        acc_out[span] += mat(act, down[...])
        acc_in[span] += mat_nt(pre_low, up[...])
    vec_scr[pl.ds(4 + step, 1)] = total

    @pl.when(step == pl.num_programs(0) - 1)
    def _():
        pl.semaphore_wait(barrier, 3)
        sums = [jnp.zeros((1, model), F32) for _ in range(4)]
        for c, span in enumerate(spans):
            resid = resid_scr[span]
            normed, scale = row_stats(resid)
            inner_grad = acc_in[span]
            wide = grad[span].astype(F32)
            resid_grad = wide + norm_back(inner_grad * as_row(gain_ref), normed, scale)
            resid_out[span] = resid_grad
            low = resid_grad.astype(BF16)
            in_scr[span] = low
            back_t[...] = mat_nt(out_w[...], low).astype(BF16)
            for r in (2, 3, 1, 0):
                grads_vm[c, r] = back_t[group_rows(r)]
                if c == 0 and r:
                    grad_copy(r).start()
            layer_out[span] = (resid + acc_out[span] + as_row(down_b)).astype(BF16)
            for i, term in enumerate((wide, resid_grad, inner_grad * normed, inner_grad)):
                sums[i] = sums[i] + jnp.sum(term, axis=0, keepdims=True)
        out_copy(3).start()
        for i in range(4):
            vec_scr[i : i + 1] = sums[i]
        for t in range(tiles):
            down_term = mat_tn(act_scr[t], grad[...])
            if direct:
                for i in range(model // share):
                    slab_vm[t * (model // share) + i, 0:share] = down_term[
                        i * share : (i + 1) * share
                    ].astype(BF16)
            else:
                down_vm[t * model : (t + 1) * model] = down_term.astype(BF16)
        out_copy(0).start()
        for t in range(0, tiles, 2):
            terms = [mat(in_t[...], pre_scr[t]), mat(in_t[...], pre_scr[t + 1])]
            if direct:
                for i in range(owners):
                    own_rows = slice(i * small, (i + 1) * small)
                    slab_vm[i, share + t * small : share + (t + 2) * small] = jnp.concatenate(
                        [term[own_rows] for term in terms], axis=0
                    ).astype(BF16)
            else:
                for u, term in enumerate(terms):
                    up_vm[:, (t + u) * model : (t + u + 1) * model] = term.astype(BF16)
        out_copy(1).start()
        out_term = mat(mixed_t[...], in_scr[...])
        fill = aligned(small + 8) - small - 8
        extra = [jnp.zeros((fill, model), F32)] if fill else []
        for i in range(owners):
            rest = jnp.concatenate(
                [out_term[i * small : (i + 1) * small], vec_scr[...]] + extra, axis=0
            ).astype(BF16)
            if direct:
                slab_vm[i, 2 * share :] = rest
            else:
                tail_vm[i] = rest
        out_copy(2).start()
        for r in (1, 2, 3):
            grad_copy(r).wait_recv()
        out_copy(4).start()
        for r in (1, 2, 3):
            grad_copy(r).wait_send()
        for i in range(5):
            out_copy(i).wait()


def block_layer(
    parts, hidden, grad, out_w, out_b, gain, shift, down_b, up_b, up, down, act_grad, devices
):
    tokens, model = hidden.shape
    ff = up.shape[1]
    steps = ff // model
    seqs = parts.shape[0]
    small, share = model // devices, ff // devices
    direct = small % 8 == 0 and share % 16 == 0
    tail_rows = aligned(small + 8)
    single = pl.Buffered(1)
    whole = lambda *shape: pl.BlockSpec(
        shape, lambda t: (0,) * len(shape), pipeline_mode=single
    )
    anywhere = pl.BlockSpec(memory_space=pl.ANY)
    unused = (16, 128)
    slab_shape, down_shape, up_shape, tail_shape = (
        ((devices, 2 * share + tail_rows, model), unused, unused, unused) if direct
        else (unused, (ff, model), (model, ff), (devices, tail_rows, model))
    )
    layer_out, resid_grad, grads, first, slab, down_grad, up_grad, tail = pl.pallas_call(
        lambda *refs: block_kernel(direct, *refs),
        grid=(steps,),
        out_shape=(
            jax.ShapeDtypeStruct((tokens, model), BF16),
            jax.ShapeDtypeStruct((tokens, model), F32),
            jax.ShapeDtypeStruct(parts.shape, BF16),
            jax.ShapeDtypeStruct((3,) + parts.shape[2:], BF16),
            jax.ShapeDtypeStruct(slab_shape, BF16),
            jax.ShapeDtypeStruct(down_shape, BF16),
            jax.ShapeDtypeStruct(up_shape, BF16),
            jax.ShapeDtypeStruct(tail_shape, BF16),
        ),
        in_specs=[
            whole(*parts.shape), whole(tokens, model), whole(tokens, model), whole(model, model),
            whole(model), whole(model), whole(model), whole(model), whole(ff),
            pl.BlockSpec((model, model), lambda t: (0, t)),
            pl.BlockSpec((model, model), lambda t: (t, 0)),
            pl.BlockSpec((None, tokens, model), lambda t: (t, 0, 0)),
        ],
        out_specs=(
            whole(tokens, model), whole(tokens, model), anywhere, anywhere, anywhere, anywhere,
            anywhere, anywhere,
        ),
        scratch_shapes=[
            pltpu.VMEM((model, tokens), BF16),
            pltpu.VMEM((tokens, model), F32),
            pltpu.VMEM((tokens, model), BF16),
            pltpu.VMEM((model, tokens), BF16),
            pltpu.VMEM((tokens, model), F32),
            pltpu.VMEM((tokens, model), F32),
            pltpu.VMEM((steps, tokens, model), BF16),
            pltpu.VMEM((steps, tokens, model), BF16),
            pltpu.VMEM((8, model), F32),
            pltpu.VMEM((1, ff), F32),
            pltpu.VMEM((model, CHUNK), BF16),
            pltpu.VMEM(slab_shape, BF16),
            pltpu.VMEM(down_shape, BF16),
            pltpu.VMEM(up_shape, BF16),
            pltpu.VMEM(tail_shape, BF16),
            pltpu.VMEM(parts.shape, BF16),
            pltpu.VMEM((3,) + parts.shape[2:], BF16),
            pltpu.SemaphoreType.DMA((3,)),
            pltpu.SemaphoreType.DMA((3,)),
            pltpu.SemaphoreType.DMA((5,)),
        ],
        compiler_params=pltpu.CompilerParams(
            vmem_limit_bytes=VMEM, collective_id=3, has_side_effects=True
        ),
        cost_estimate=pl.CostEstimate(
            flops=26_000_000_000, bytes_accessed=30_000_000, transcendentals=0
        ),
        name="block_layer",
    )(parts, hidden, grad, out_w, out_b, gain, shift, down_b, up_b, up, down, act_grad)
    if not direct:
        fit = lambda a: jnp.pad(a, ((0, 0), (0, aligned(a.shape[1]) - a.shape[1]), (0, 0)))
        down_grad = fit(down_grad.reshape(devices, share, model))
        up_grad = up_grad.reshape(devices, small, ff // model, model).transpose(0, 2, 1, 3)
        up_grad = fit(up_grad.reshape(devices, ff // model * small, model))
        slab = jnp.concatenate([down_grad, up_grad, tail], axis=1)
    return layer_out, resid_grad, grads, first, slab


def attend_back_kernel(
    dp_size, x_ref, grads_ref, first_ref, weight, draws_ref, hot_ref, proj, state_ref, mixed_ref, den_ref,
    soft_ref, phi_q_ref, phi_k_ref, slab_any,
    attn_out, ring_out, proj_out,
    grad_scr, num_scr, value_scr, score_scr, exact_scr, proj_scr,
    grad_land, near_send, near_land, far_keep, far_send, far_land,
    mine, met, ring_land, cross_land,
    weight_acc, own_send, pair_land, own_mid, own_land, part_send, part_land,
    grad_sems, near_sems, far_sems, mine_sem, met_send, met_sems, ring_send, ring_sems, cross_sems,
    pair_sems, own_send_sem, own_sems,
    part_sems,
):
    s, h = pl.program_id(0), pl.program_id(1)
    seqs, heads = pl.num_programs(0), pl.num_programs(1)
    rows, model = x_ref.shape[1], x_ref.shape[2]
    head_count = proj_scr.shape[0] // (3 * HD)
    width = head_count * HD
    total = GROUP * rows
    root = 1.0 / math.sqrt(HD)
    own, me = lax.axis_index("feat"), lax.axis_index("dp")
    own_x, own_core = own // 2, own % 2
    near, across = {"feat": partner(own, 1)}, {"feat": partner(own, 2)}
    last = (s == seqs - 1) & (h == heads - 1)

    def grad_copy(q, r):
        return remote(
            grads_ref.at[q, r], grad_land.at[q - 1, r - 1], grad_sems.at[0, q - 1, r - 1],
            grad_sems.at[1, q - 1, r - 1], {"feat": partner(own, r)},
        )

    def near_copy(q, i):
        return remote(
            near_send.at[i], near_land.at[q, i], near_sems.at[0, q, i], near_sems.at[1, q, i], near
        )

    def far_copy(q):
        return remote(far_send, far_land.at[q], far_sems.at[0, q], far_sems.at[1, q], across)

    half = dp_size // 2
    parity, pair = lax.rem(me, 2), lax.div(me, 2)
    spot = pair + parity * (dp_size - 1 - 2 * pair)

    def at_spot(p):
        p = lax.rem(p + dp_size, dp_size)
        upper = lax.div(p, half)
        return 2 * p + upper * (2 * dp_size - 1 - 4 * p)

    places = ({"dp": at_spot(spot + 1)}, {"dp": at_spot(spot - 1)})

    def chunk(k, way):
        return at_spot(spot - 1 - k) if way == 0 else at_spot(spot + 1 + k)

    def mine_copy(k, way, owner):
        return pltpu.make_async_copy(
            slab_any.at[owner + own_core], mine.at[k, way], mine_sem.at[k, way]
        )

    def met_copy(k, way, owner):
        return remote(
            slab_any.at[owner + 1 - own_core], met.at[k, way], met_send, met_sems.at[k, way], near
        )

    cut = aligned(mine.shape[2] // 2)
    halves = (pl.ds(0, cut), pl.ds(cut, mine.shape[2] - cut))

    def ring_copy(k, way, part):
        return remote(
            mine.at[k, way, halves[part]], ring_land.at[k, way, halves[part]], ring_send,
            ring_sems.at[k, way, part], places[way],
        )

    def cross_copy(part):
        return remote(
            mine.at[dp_size - 1, 1 - own_x, halves[part]], cross_land.at[halves[part]],
            cross_sems.at[0, part], cross_sems.at[1, part], across,
        )

    def begin_pieces(k):
        for way in range(2):
            owner = chunk(k, way) * GROUP + 2 * way
            met_copy(k, way, owner).start()
            mine_copy(k, way, owner).start()

    def ring_step(k, part):
        span = halves[part]
        if part == 0:

            @pl.when(k + 2 < dp_size)
            def _():
                begin_pieces(k + 2)

        @pl.when(k < dp_size)
        def _():
            for way in range(2):
                if part == 0:
                    mine_copy(k, way, 0).wait()
                    met_copy(k, way, 0).wait_recv()

                @pl.when(k == 0)
                def _():
                    base = mine[k, way, span].astype(F32) + met[k, way, span].astype(F32)
                    mine[k, way, span] = base.astype(BF16)

                @pl.when(k > 0)
                def _():
                    ring_copy(k - 1, way, part).wait_recv()
                    base = mine[k, way, span].astype(F32) + met[k, way, span].astype(F32)
                    base = base + ring_land[k - 1, way, span].astype(F32)
                    mine[k, way, span] = base.astype(BF16)

                @pl.when(k < dp_size - 1)
                def _():
                    ring_copy(k, way, part).start()

            @pl.when(k == dp_size - 1)
            def _():
                cross_copy(part).start()

        @pl.when(k == dp_size)
        def _():
            cross_copy(part).wait_recv()
            ring_out[span] = mine[dp_size - 1, own_x, span].astype(F32) + cross_land[span].astype(F32)

    def ring_turn(part):
        turn = s * heads + h
        count = seqs * heads
        steps = dp_size + 1

        def body(k, carry):
            ring_step(k, part)
            return carry

        lax.fori_loop(lax.div(turn * steps, count), lax.div((turn + 1) * steps, count), body, 0)

    mate = me + 1 - 2 * parity

    def pair_copy(q):
        return remote(
            own_send.at[q, 1 - parity], pair_land.at[q], pair_sems.at[0, q], pair_sems.at[1, q],
            {"dp": mate},
        )

    def own_copy(q, k):
        to = lax.rem(pair + k, half)
        return remote(
            own_mid.at[q, to], own_land.at[q, k], own_send_sem, own_sems.at[q, k],
            {"dp": 2 * to + parity},
        )

    base = model // dp_size

    def folded(values):
        middle = values.shape[0] // 2
        return jnp.concatenate([values[0:middle], values[middle:]], axis=1)

    def begin_own(q):
        turned = weight_acc[pl.ds(pl.multiple_of(q * 3 * HD, 3 * HD), 3 * HD)].T
        biases = turned[model : model + 16]
        blank = own_send.shape[3] - base - base // 2 - 16
        extra = [jnp.zeros((blank, 2 * HD), F32)] if blank else []
        for c in range(dp_size):
            block = turned[c * base : (c + 1) * base]
            own_send[q, c % 2, c // 2] = jnp.concatenate(
                [
                    block[:, 0 : 2 * HD], folded(block[:, 2 * HD :]), biases[0:8, 0 : 2 * HD],
                    folded(biases[:, 2 * HD :]),
                ] + extra,
                axis=0,
            ).astype(BF16)
        pair_copy(q).start()

    def relay_own(q):
        pair_copy(q).wait_recv()
        own_mid[q] = (own_send[q, parity].astype(F32) + pair_land[q].astype(F32)).astype(BF16)

        def start(k, carry):
            own_copy(q, k).start()
            return carry

        lax.fori_loop(1, half, start, 0)

    def part_copy(r):
        other = partner(own, r)
        return remote(
            part_send.at[other], part_land.at[r - 1], part_sems.at[0, r - 1],
            part_sems.at[1, r - 1], {"feat": other},
        )

    def seq_span(q):
        return pl.ds(pl.multiple_of(q * rows, rows), rows)

    def add_near(q):
        near_copy(q, 1).wait_recv()

        @pl.when(q > 0)
        def _():
            far_copy(q - 1).wait_send()

        far_send[...] = (far_keep[1] + near_land[q, 1].astype(F32)).astype(BF16)
        far_copy(q).start()
        near_copy(q, 0).wait_recv()
        attn_out[seq_span(q)] = far_keep[0] + near_land[q, 0].astype(F32)

    def finish(q):
        far_copy(q).wait_recv()
        span = seq_span(q)
        attn_out[span] = attn_out[span] + far_land[q].astype(F32)

    @pl.when((s == 0) & (h == 0))
    def _():
        barrier = pltpu.get_barrier_semaphore()
        for r in (1, 2, 3):
            pl.semaphore_signal(
                barrier, inc=1, device_id={"feat": partner(own, r)}, device_id_type=MESH
            )

        def greet(k, carry):
            pl.semaphore_signal(
                barrier, inc=1, device_id={"dp": lax.rem(me + k, dp_size)}, device_id_type=MESH
            )
            return carry

        lax.fori_loop(1, dp_size, greet, 0)
        pl.semaphore_wait(barrier, 3 + dp_size - 1)
        for q in range(1, near_land.shape[0]):
            for r in (2, 3, 1):
                grad_copy(q, r).start()
        for k in range(2):
            begin_pieces(k)
        weight_acc[...] = jnp.zeros_like(weight_acc)

    @pl.when(h == 0)
    def _():
        grad_scr[:, 0:rows] = grads_ref[s, 0].astype(F32)

        @pl.when(s == 0)
        def _():
            for r in (1, 2, 3):
                grad_scr[:, r * rows : (r + 1) * rows] = first_ref[r - 1].astype(F32)

        @pl.when(s > 0)
        def _():
            for r in (1, 2, 3):
                grad_copy(s, r).wait_recv()
                grad_scr[:, r * rows : (r + 1) * rows] = grad_land[s - 1, r - 1].astype(F32)

    query = proj[head_rows(h, 0, head_count)]
    key = proj[head_rows(h, 1, head_count)]
    value = proj[head_rows(h, 2, head_count)]
    draws = draws_ref[...]
    draws_ext = jnp.concatenate([draws, jnp.ones((16, FEAT), BF16)], axis=0)
    hot = hot_ref[...]
    away_wide = away_marks(hot)
    away = away_wide.astype(BF16)
    inverse = 1.0 / den_ref[0:1]
    head_grad = grad_scr[pl.ds(pl.multiple_of(h * HD, HD), HD)]
    grad_num = (head_grad * inverse).astype(BF16)
    grad_den = -jnp.sum(head_grad * mixed_ref[...], axis=0, keepdims=True) * inverse
    den_rows = jnp.broadcast_to(grad_den, (16, total)).astype(BF16)
    spread_grad = jnp.concatenate(spread(grad_num, hot) + [den_rows * hot], axis=0)
    spread_value = jnp.concatenate(spread(value, away) + [away], axis=0)

    phi_q, phi_k = phi_q_ref[...], phi_k_ref[...]
    state_grad = mat_nt(spread_grad, phi_q).astype(BF16)
    phi_q_grad = mat_tn(state_ref[...], spread_grad)
    phi_k_grad = mat_tn(state_grad, spread_value)
    value_low = mat(state_grad[0 : NBUCK * HD], phi_k)
    scaled_q = (phi_q_grad * phi_q.astype(F32)).astype(BF16)
    back_q = mat(draws_ext, scaled_q)
    scaled_k = (phi_k_grad * phi_k.astype(F32)).astype(BF16)
    back_k = mat(draws_ext, scaled_k)
    value_grad = pick(value_low, away_wide)
    query_grad = back_q[0:HD] - query.astype(F32) * (back_q[HD : HD + 1] * root)
    key_grad = back_k[0:HD] - key.astype(F32) * (back_k[HD : HD + 1] * root)

    ring_turn(0)
    one = (lax.broadcasted_iota(jnp.int32, hot.shape, 0) < 1).astype(F32).astype(BF16)
    num_scr[...] = jnp.concatenate([grad_num, den_rows], axis=0)
    value_scr[...] = jnp.concatenate([value, one], axis=0).astype(F32).T.astype(BF16)

    later = mat(value_scr[...], num_scr[:, 0:CHUNK])
    for c in range(total // CHUNK):
        cols = slice(c * CHUNK, (c + 1) * CHUNK)
        ahead = slice((c + 1) * CHUNK, (c + 2) * CHUNK)
        score = later
        later = mat(value_scr[...], num_scr[:, ahead]) if ahead.stop <= total else None
        score = (score * soft_ref[:, cols].astype(F32)).astype(BF16)
        score_scr[:, cols] = score
        exact_scr[:, cols] = mat(proj[head_rows(h, 1, head_count)], score)
    query_grad = query_grad + exact_scr[...] * root
    key_grad = key_grad + mat_nt(query, score_scr[...]) * root
    value_grad = value_grad + mat_nt(grad_num, soft_ref[...])
    wide_grad = jnp.concatenate([query_grad, key_grad, value_grad], axis=0)
    low_grad = wide_grad.astype(BF16)
    for kind in range(3):
        proj_scr[head_rows(h, kind, head_count)] = low_grad[kind * HD : (kind + 1) * HD]
    weight_grad = mat(low_grad[:, 0:rows], x_ref[0])
    for r in (1, 2, 3):
        weight_grad = weight_grad + mat(low_grad[:, r * rows : (r + 1) * rows], x_ref[r])
    span = pl.ds(pl.multiple_of(h * 3 * HD, 3 * HD), 3 * HD)
    weight_acc[span, 0:model] += weight_grad
    weight_acc[span, model:] += jnp.broadcast_to(
        jnp.sum(wide_grad, axis=1, keepdims=True), (3 * HD, 128)
    )

    @pl.when(s == seqs - 1)
    def _():
        begin_own(h)

        @pl.when(h > 0)
        def _():
            relay_own(h - 1)

    @pl.when((s > 0) & (h == 0))
    def _():
        add_near(s - 1)

    @pl.when(h == heads - 1)
    def _():
        @pl.when(s > 0)
        def _():
            for i in range(2):
                near_copy(s - 1, i).wait_send()

        for r in (3, 1, 2, 0):
            term = mat_tn(proj_scr[:, r * rows : (r + 1) * rows], weight[...])
            if r % 2:
                near_send[r // 2] = term.astype(BF16)
                near_copy(s, r // 2).start()
            else:
                far_keep[r // 2] = term

    ring_turn(1)

    @pl.when(last)
    def _():
        add_near(s)
        relay_own(h)
        for q in range(near_land.shape[0] - 1):
            finish(q)

        sums = []
        for q in range(head_count):

            def arrive(k, carry):
                own_copy(q, k).wait_recv()
                return carry + own_land[q, k].astype(F32)

            sums.append(lax.fori_loop(1, half, arrive, own_mid[q, pair].astype(F32)))
        blocks, biases = [], []
        end = base + base // 2
        for total_sum in sums:
            value_rows = total_sum[base:end]
            value_rows = jnp.concatenate([value_rows[:, 0:HD], value_rows[:, HD:]], axis=0)
            blocks += [total_sum[0:base], value_rows]
            biases += [total_sum[end : end + 1], total_sum[end + 8 : end + 9, 0:HD]]
        joined = jnp.concatenate(blocks, axis=1)
        small = base // GROUP
        fill = jnp.broadcast_to(
            jnp.concatenate(biases, axis=1), (part_send.shape[1] - small, joined.shape[1])
        )
        for a in range(GROUP):
            part_send[a] = jnp.concatenate(
                [joined[a * small : (a + 1) * small], fill], axis=0
            ).astype(BF16)
        for r in (2, 3, 1):
            part_copy(r).start()
        finish(s)
        proj_out[own] = part_send[own].astype(F32)
        for r in (1, 2, 3):
            part_copy(r).wait_recv()
            proj_out[partner(own, r)] = part_land[r - 1].astype(F32)

        for i in range(2):
            near_copy(s, i).wait_send()
        far_copy(s).wait_send()
        for r in (1, 2, 3):
            part_copy(r).wait_send()
        for part in range(2):
            cross_copy(part).wait_send()
        for q in range(1, near_land.shape[0]):
            for r in (1, 2, 3):
                grad_copy(q, r).wait_send()
        for q in range(head_count):
            pair_copy(q).wait_send()
        every = pl.ds(0, half - 1)
        if half > 1:
            remote(
                own_mid.at[:, every], own_land.at[:, every], own_send_sem, own_sems.at[0, 0],
                {"dp": mate},
            ).wait_send()
        remote(
            mine.at[pl.ds(0, dp_size - 1)], ring_land, ring_send, ring_sems.at[0, 0, 0], places[0]
        ).wait_send()
        remote(mine, met, met_send, met_sems.at[0, 0], near).wait_send()


def attend_back(
    dp_size, parts, grads, first, weight, draws, hot, proj, state, mixed, den, soft, phi_q, phi_k,
    slab,
):
    seqs, _, rows, model = parts.shape
    heads = draws.shape[0]
    width = heads * HD
    total = GROUP * rows
    n = dp_size
    ring_rows = slab.shape[1]
    own_rows = aligned(model // n + model // n // 2 + 16)
    part_rows = aligned(model // (n * GROUP) + 1)
    single = pl.Buffered(1)
    whole = lambda *shape: pl.BlockSpec(
        shape, lambda s, h: (0,) * len(shape), pipeline_mode=single
    )
    mode = single if n > 16 else None
    by_seq = lambda *shape: pl.BlockSpec(
        (None,) + shape, lambda s, h: (s,) + (0,) * len(shape), pipeline_mode=mode
    )
    by_head = lambda *shape: pl.BlockSpec(
        (None, None) + shape, lambda s, h: (s, h) + (0,) * len(shape), pipeline_mode=mode
    )
    anywhere = pl.BlockSpec(memory_space=pl.ANY)
    dma = pltpu.SemaphoreType.DMA
    return pl.pallas_call(
        lambda *refs: attend_back_kernel(dp_size, *refs),
        grid=(seqs, heads),
        out_shape=(
            jax.ShapeDtypeStruct((seqs * rows, model), F32),
            jax.ShapeDtypeStruct((ring_rows, model), F32),
            jax.ShapeDtypeStruct((GROUP, part_rows, 3 * width), F32),
        ),
        in_specs=[
            by_seq(GROUP, rows, model), whole(*grads.shape), whole(*first.shape),
            whole(3 * width, model),
            pl.BlockSpec((None, HD, FEAT), lambda s, h: (h, 0, 0)),
            by_seq(16, total), by_seq(3 * width, total), by_head(STATES, FEAT), by_head(HD, total),
            by_head(8, total), by_head(total, total), by_head(FEAT, total), by_head(FEAT, total),
            anywhere,
        ],
        out_specs=(
            whole(seqs * rows, model), whole(ring_rows, model), whole(GROUP, part_rows, 3 * width),
        ),
        scratch_shapes=[
            pltpu.VMEM((width, total), F32),
            pltpu.VMEM((HD + 16, total), BF16),
            pltpu.VMEM((total, HD + 16), BF16),
            pltpu.VMEM((total, total), BF16),
            pltpu.VMEM((HD, total), F32),
            pltpu.VMEM((3 * width, total), BF16),
            pltpu.VMEM((seqs - 1, 3, width, rows), BF16),
            pltpu.VMEM((2, rows, model), BF16),
            pltpu.VMEM((seqs, 2, rows, model), BF16),
            pltpu.VMEM((2, rows, model), F32),
            pltpu.VMEM((rows, model), BF16),
            pltpu.VMEM((seqs, rows, model), BF16),
            pltpu.VMEM((n, 2, ring_rows, model), BF16),
            pltpu.VMEM((n, 2, ring_rows, model), BF16),
            pltpu.VMEM((n - 1, 2, ring_rows, model), BF16),
            pltpu.VMEM((ring_rows, model), BF16),
            pltpu.VMEM((3 * width, model + 128), F32),
            pltpu.VMEM((heads, 2, n // 2, own_rows, 2 * HD), BF16),
            pltpu.VMEM((heads, n // 2, own_rows, 2 * HD), BF16),
            pltpu.VMEM((heads, n // 2, own_rows, 2 * HD), BF16),
            pltpu.VMEM((heads, n // 2, own_rows, 2 * HD), BF16),
            pltpu.VMEM((GROUP, part_rows, 3 * width), BF16),
            pltpu.VMEM((3, part_rows, 3 * width), BF16),
            dma((2, seqs - 1, 3)),
            dma((2, seqs, 2)),
            dma((2, seqs)),
            dma((n, 2)),
            dma,
            dma((n, 2)),
            dma,
            dma((n - 1, 2, 2)),
            dma((2, 2)),
            dma((2, heads)),
            dma,
            dma((heads, n // 2)),
            dma((2, 3)),
        ],
        compiler_params=pltpu.CompilerParams(
            vmem_limit_bytes=VMEM + (3 * 1024 * 1024 if n > 16 else 0), collective_id=2, has_side_effects=True
        ),
        cost_estimate=pl.CostEstimate(
            flops=48_000_000_000, bytes_accessed=40_000_000, transcendentals=0
        ),
        name="attend_back",
    )(
        parts, grads, first, weight, draws, hot, proj, state, mixed, den, soft, phi_q, phi_k, slab,
    )


def finish_kernel(
    starts, heads, attn_grad, resid_grad, hidden, sums, proj_sums, weight_any, gain_ref, shift_ref,
    input_out, norm1_gain_out, norm1_bias_out, qkv_out, qkv_bias_out, out_out, out_bias_out,
    norm2_gain_out, norm2_bias_out, up_out, up_bias_out, down_out, down_bias_out,
    weight_vm, weight_sem,
):
    gain, shift = as_row(gain_ref), as_row(shift_ref)
    index = lax.axis_index("dp") * GROUP + lax.axis_index("feat")
    small, model = out_out.shape
    window = weight_vm.shape[0]
    begin = jnp.minimum(lax.div(index * small, 16) * 16, model - window)
    weight_copy = pltpu.make_async_copy(
        weight_any.at[pl.ds(pl.multiple_of(begin, 16), window)], weight_vm, weight_sem
    )

    @pl.when(pl.program_id(0) == 0)
    def _():
        weight_copy.start()

    normed, scale = row_stats(hidden[...].astype(F32))
    input_out[...] = resid_grad[...] + norm_back(attn_grad[...] * gain, normed, scale)

    @pl.when(pl.program_id(0) == 0)
    def _():
        share = down_out.shape[0]
        ff = up_out.shape[1]

        def own(row, size):
            length = row.shape[1]
            wide = jnp.broadcast_to(row, (8, length))
            back = lax.rem(length - lax.rem(index * size, length), length)
            return pltpu.roll(wide, back, 1)[0:1, 0:size]

        down_out[...] = sums[0:share]
        first = starts[0]
        up_out[...] = jnp.concatenate(
            [sums[first + i * small : first + (i + 1) * small] for i in range(ff // model)], axis=1
        )
        first = starts[1]
        out_out[...] = sums[first : first + small]
        totals = first + small
        for i, out in enumerate((down_bias_out, out_bias_out, norm2_gain_out, norm2_bias_out)):
            out[...] = own(sums[totals + i : totals + i + 1], small).reshape(small)
        per_row = model // share
        level = index // per_row
        row = jnp.zeros((1, model), F32)
        for i in range(ff // model):
            row = jnp.where(level == i, sums[totals + 4 + i : totals + 5 + i], row)
        up_bias_out[...] = own(row, share).reshape(share)

        pieces = []
        for kind in range(3):
            for f in range(GROUP):
                for h in range(heads):
                    lanes = slice((h * 3 + kind) * HD, (h * 3 + kind + 1) * HD)
                    pieces.append(proj_sums[f, 0 : small + 1, lanes])
        grid = jnp.concatenate(pieces, axis=1)
        weight_sum, bias_sum = grid[0:small], grid[small : small + 1]
        qkv_out[...] = weight_sum
        qkv_bias_out[...] = own(bias_sum, 3 * small).reshape(3 * small)
        weight_copy.wait()
        near_rows = weight_vm[...].astype(F32)
        step = math.gcd(small, 16)
        wide = near_rows[0:small]
        for offset in range(step, window - small + 1, step):
            wide = jnp.where(
                index * small - begin == offset, near_rows[offset : offset + small], wide
            )

        def to_row(column):
            column = jnp.concatenate(
                [column, jnp.zeros((-small % 128, 1), F32)], axis=0
            )
            return jnp.broadcast_to(column, (column.shape[0], 128)).T[0:1, 0:small]

        bias_grad = to_row(jnp.sum(wide * bias_sum, axis=1, keepdims=True))
        gain_grad = to_row(jnp.sum(wide * weight_sum, axis=1, keepdims=True))
        norm1_bias_out[...] = bias_grad.reshape(small)
        gain_grad = (gain_grad - own(shift, small) * bias_grad) / own(gain, small)
        norm1_gain_out[...] = gain_grad.reshape(small)


def finish_all(
    attn_grad, resid_grad, hidden, sums, proj_sums, weight, gain, shift, devices, ff, heads,
):
    seqs, rows, model = hidden.shape
    small, share = model // devices, ff // devices
    starts = (aligned(share), 2 * aligned(share))
    whole = lambda *shape: pl.BlockSpec(shape, lambda s: (0,) * len(shape))
    by_seq = pl.BlockSpec((rows, model), lambda s: (s, 0))
    shapes = (
        (small,), (small,), (small, 3 * model), (3 * small,), (small, model), (small,), (small,),
        (small,), (small, ff), (share,), (share, model), (small,),
    )
    return pl.pallas_call(
        lambda *refs: finish_kernel(starts, heads, *refs),
        grid=(seqs,),
        out_shape=(jax.ShapeDtypeStruct((seqs * rows, model), F32),)
        + tuple(jax.ShapeDtypeStruct(shape, F32) for shape in shapes),
        in_specs=[
            by_seq, by_seq, pl.BlockSpec((None, rows, model), lambda s: (s, 0, 0)),
            whole(*sums.shape), whole(*proj_sums.shape), pl.BlockSpec(memory_space=pl.ANY), whole(model),
            whole(model),
        ],
        out_specs=(by_seq,) + tuple(whole(*shape) for shape in shapes),
        scratch_shapes=[
            pltpu.VMEM((aligned(small) + 16, 3 * model), BF16), pltpu.SemaphoreType.DMA,
        ],
        compiler_params=pltpu.CompilerParams(vmem_limit_bytes=VMEM),
        name="finish_all",
    )(attn_grad, resid_grad, hidden, sums, proj_sums, weight, gain, shift)


def per_device(
    hidden_in, norm1_gain, norm1_bias, qkv_weight, qkv_bias, feature_draws, out_weight, out_bias,
    norm2_gain, norm2_bias, up_weight, up_bias, down_weight, down_bias, block_bucket, out_grad,
):
    seqs, rows, model = hidden_in.shape
    ff = up_weight.shape[1]
    dp_size = lax.axis_size("dp")
    devices = dp_size * GROUP
    heads = feature_draws.shape[0] // GROUP
    flat = (seqs * rows, model)

    (
        parts, mixed_parts, act_grad, proj, state, mixed, den, hot, own_weight, own_draws, soft,
        phi_q, phi_k,
    ) = attend(
        block_bucket, hidden_in, norm1_gain, norm1_bias, qkv_bias, qkv_weight, feature_draws,
        out_grad, down_weight,
    )
    layer_out, resid_grad, grads, first, slab = block_layer(
        mixed_parts, hidden_in.reshape(flat), out_grad.reshape(flat), out_weight, out_bias,
        norm2_gain, norm2_bias, down_bias, up_bias, up_weight, down_weight, act_grad, devices,
    )
    attn_grad, sums, proj_sums = attend_back(
        dp_size, parts, grads, first, own_weight, own_draws, hot, proj, state, mixed, den, soft,
        phi_q, phi_k, slab,
    )
    (
        input_grad, norm1_gain_sum, norm1_bias_sum, qkv_weight_sum, qkv_bias_sum, out_weight_sum,
        out_bias_sum, norm2_gain_sum, norm2_bias_sum, up_sum, up_bias_sum, down_sum, down_bias_sum,
    ) = finish_all(
        attn_grad, resid_grad, hidden_in, sums, proj_sums, qkv_weight, norm1_gain, norm1_bias,
        devices, ff, heads,
    )
    return (
        layer_out.reshape(hidden_in.shape), input_grad.reshape(hidden_in.shape), norm1_gain_sum,
        norm1_bias_sum, qkv_weight_sum, qkv_bias_sum, out_weight_sum, out_bias_sum, norm2_gain_sum,
        norm2_bias_sum, up_sum, up_bias_sum, down_sum, down_bias_sum,
    )


def solution(mesh):
    both = ("dp", "feat")
    rows = P("dp", "feat", None)
    in_specs = (
        rows, P(), P(), P(), P(), P(None, None, "feat"), P(), P(), P(), P(), P(), P(), P(), P(),
        P("dp", None, None), rows,
    )
    out_specs = (
        rows, rows, P(both), P(both), P(both, None), P(both), P(both, None), P(both), P(both),
        P(both), P(both, None), P(both), P(both, None), P(both),
    )
    return jax.shard_map(
        per_device, mesh=mesh, in_specs=in_specs, out_specs=out_specs, check_vma=False
    )
```

profile of v0, /device:TPU:0, one launch (start us, length us, event | category | flops | bytes accessed | tf_op | source)
XLA Modules:
  0.0 191.2 jit_solution(4040987830132369120)
XLA Ops:
  0.6 1.4 copy.30.bucket
  2.0 53.1 %attend.1 = (bf16[3,4,256,768]{3,2,1,0:T(8,128)(2,1)}, bf16[3,4,192,256]{3,2,1,0:T(8,128)(2,1)}, bf16[4,768,768]{2,1,0:T(8,128)(2,1)}, bf16[3,576,1024]{2,1,0:T(...) custom-call(s32[3,16,1]{2,1,0:T(8,128)} %copy.30.bucket, ...), custom_call_target="tpu_custom_call" | custom-call | flops 24000000000 | bytes 20000000 | tf_op jit(solution)/shard_map/attend/pallas_call | solution.py:309
  55.1 36.1 %block_layer.1 = (bf16[768,768]{1,0:T(8,128)(2,1)}, f32[768,768]{1,0:T(8,128)}, bf16[3,4,192,256]{3,2,1,0:T(8,128)(2,1)}, bf16[3,192,256]{2,1,0:T(8,128)(2,1)}, ...) custom-call(bf16[3,4,192,256]{3,2,1,0:T(8,128)(2,1)} %get-tuple-elem, ...), custom_call_target="tpu_custom_call" | custom-call | flops 25999998976 | bytes 30000000 | tf_op jit(solution)/shard_map/block_layer/pallas_call | solution.py:541
  91.2 91.4 %attend_back.1 = (f32[768,768]{1,0:T(8,128)}, f32[224,768]{1,0:T(8,128)}, f32[4,32,576]{2,1,0:T(8,128)}) custom-call(bf16[3,4,256,768]{3,2,1,0:T(8,128)(2,1)} %get-tuple-element.51.refs_0_, bf16[3,4,192,256]{3,2,1,0:T(8,128)(2,1)} %get-tuple-element.52.refs_1_, bf16[3,192,256]{2,1,0:T(8,128)(2,1)} %get-tuple-element.53.refs_2_, ...), custom_call_target="tpu_custom_call" | custom-call | flops 48000000000 | bytes 40000000 | tf_op jit(solution)/shard_map/attend_back/pallas_call | solution.py:1026
  182.7 0.0 copy-start
  182.7 7.5 %finish_all.1 = (f32[768,768]{1,0:T(8,128)}, f32[24]{0:T(128)}, f32[24]{0:T(128)}, f32[24,2304]{1,0:T(8,128)}, f32[72]{0:T(128)}, /*index=5*/f32[24,768]{1,0:T(8...) custom-call(f32[768,768]{1,0:T(8,128)} %get-tuple-element.65.refs_0_, ...), custom_call_target="tpu_custom_call" | custom-call | tf_op jit(solution)/shard_map/finish_all/pallas_call | solution.py:1189
  190.2 0.0 copy-done
  190.2 1.0 copy.32
Async XLA Ops:
  182.7 7.5 %copy-start = (bf16[768,768]{1,0:T(8,128)(2,1)S(1)}, bf16[768,768]{1,0:T(8,128)(2,1)}, u32[]{:S(2)}) copy-start(bf16[768,768]{1,0:T(8,128)(2,1)} %get-tuple-element.50) | copy-start | bytes 3538948
where the time goes:
time: 191 us
  Pallas kernels  188 us (98%)
  local copies, waits for them, and re-layouts  2.4 us (1%)
    pallas_call x1, Pallas kernels, attend_back(): pl.pallas_call(lambda *refs: attend_back_kernel(dp_size, *refs), grid=(se...  91.4 us
    pallas_call x1, Pallas kernels, attend(): pl.pallas_call(attend_kernel, grid=(seqs, heads), out_shape=(jax.ShapeDty...  53.1 us
    pallas_call x1, Pallas kernels, block_layer(): pl.pallas_call(lambda *refs: block_kernel(direct, *refs), grid=(steps,),...  36.1 us
    pallas_call x1, Pallas kernels, finish_all(): pl.pallas_call(lambda *refs: finish_kernel(starts, heads, *refs), grid=(s...  7.46 us

commit v1 on v0

--- a/solution.py
+++ b/solution.py
@@ -701,15 +701,13 @@
 
                 @pl.when(k == 0)
                 def _():
-                    base = mine[k, way, span].astype(F32) + met[k, way, span].astype(F32)
-                    mine[k, way, span] = base.astype(BF16)
+                    mine[k, way, span] = mine[k, way, span] + met[k, way, span]
 
                 @pl.when(k > 0)
                 def _():
                     ring_copy(k - 1, way, part).wait_recv()
-                    base = mine[k, way, span].astype(F32) + met[k, way, span].astype(F32)
-                    base = base + ring_land[k - 1, way, span].astype(F32)
-                    mine[k, way, span] = base.astype(BF16)
+                    chip = mine[k, way, span] + met[k, way, span]
+                    mine[k, way, span] = chip + ring_land[k - 1, way, span]
 
                 @pl.when(k < dp_size - 1)
                 def _():
@@ -868,9 +866,9 @@
     phi_q_grad = mat_tn(state_ref[...], spread_grad)
     phi_k_grad = mat_tn(state_grad, spread_value)
     value_low = mat(state_grad[0 : NBUCK * HD], phi_k)
-    scaled_q = (phi_q_grad * phi_q.astype(F32)).astype(BF16)
+    scaled_q = phi_q_grad.astype(BF16) * phi_q
     back_q = mat(draws_ext, scaled_q)
-    scaled_k = (phi_k_grad * phi_k.astype(F32)).astype(BF16)
+    scaled_k = phi_k_grad.astype(BF16) * phi_k
     back_k = mat(draws_ext, scaled_k)
     value_grad = pick(value_low, away_wide)
     query_grad = back_q[0:HD] - query.astype(F32) * (back_q[HD : HD + 1] * root)
@@ -887,7 +885,7 @@
         ahead = slice((c + 1) * CHUNK, (c + 2) * CHUNK)
         score = later
         later = mat(value_scr[...], num_scr[:, ahead]) if ahead.stop <= total else None
-        score = (score * soft_ref[:, cols].astype(F32)).astype(BF16)
+        score = score.astype(BF16) * soft_ref[:, cols]
         score_scr[:, cols] = score
         exact_scr[:, cols] = mat(proj[head_rows(h, 1, head_count)], score)
     query_grad = query_grad + exact_scr[...] * root

time: 191 us -> 191 us (level)
  no operation moved by 1% of the time
where the time goes in v1:
time: 191 us
  Pallas kernels  188 us (98%)
  local copies, waits for them, and re-layouts  2.4 us (1%)
    pallas_call x1, Pallas kernels, attend_back(): pl.pallas_call(lambda *refs: attend_back_kernel(dp_size, *refs), grid=(se...  91.4 us
    pallas_call x1, Pallas kernels, attend(): pl.pallas_call(attend_kernel, grid=(seqs, heads), out_shape=(jax.ShapeDty...  53.1 us
    pallas_call x1, Pallas kernels, block_layer(): pl.pallas_call(lambda *refs: block_kernel(direct, *refs), grid=(steps,),...  36.1 us
    pallas_call x1, Pallas kernels, finish_all(): pl.pallas_call(lambda *refs: finish_kernel(starts, heads, *refs), grid=(s...  7.46 us

profile of v1, /device:TPU:0, one launch (start us, length us, event | category | flops | bytes accessed | tf_op | source)
XLA Modules:
  0.0 191.1 jit_solution(3393651966747673411)
XLA Ops:
  0.6 1.4 copy.30.bucket
  2.0 53.1 %attend.1 = (bf16[3,4,256,768]{3,2,1,0:T(8,128)(2,1)}, bf16[3,4,192,256]{3,2,1,0:T(8,128)(2,1)}, bf16[4,768,768]{2,1,0:T(8,128)(2,1)}, bf16[3,576,1024]{2,1,0:T(...) custom-call(s32[3,16,1]{2,1,0:T(8,128)} %copy.30.bucket, ...), custom_call_target="tpu_custom_call" | custom-call | flops 24000000000 | bytes 20000000 | tf_op jit(solution)/shard_map/attend/pallas_call | solution.py:309
  55.1 36.1 %block_layer.1 = (bf16[768,768]{1,0:T(8,128)(2,1)}, f32[768,768]{1,0:T(8,128)}, bf16[3,4,192,256]{3,2,1,0:T(8,128)(2,1)}, bf16[3,192,256]{2,1,0:T(8,128)(2,1)}, ...) custom-call(bf16[3,4,192,256]{3,2,1,0:T(8,128)(2,1)} %get-tuple-elem, ...), custom_call_target="tpu_custom_call" | custom-call | flops 25999998976 | bytes 30000000 | tf_op jit(solution)/shard_map/block_layer/pallas_call | solution.py:541
  91.2 91.4 %attend_back.1 = (f32[768,768]{1,0:T(8,128)}, f32[224,768]{1,0:T(8,128)}, f32[4,32,576]{2,1,0:T(8,128)}) custom-call(bf16[3,4,256,768]{3,2,1,0:T(8,128)(2,1)} %get-tuple-element.51.refs_0_, bf16[3,4,192,256]{3,2,1,0:T(8,128)(2,1)} %get-tuple-element.52.refs_1_, bf16[3,192,256]{2,1,0:T(8,128)(2,1)} %get-tuple-element.53.refs_2_, ...), custom_call_target="tpu_custom_call" | custom-call | flops 48000000000 | bytes 40000000 | tf_op jit(solution)/shard_map/attend_back/pallas_call | solution.py:1024
  182.6 0.0 copy-start
  182.6 7.5 %finish_all.1 = (f32[768,768]{1,0:T(8,128)}, f32[24]{0:T(128)}, f32[24]{0:T(128)}, f32[24,2304]{1,0:T(8,128)}, f32[72]{0:T(128)}, /*index=5*/f32[24,768]{1,0:T(8...) custom-call(f32[768,768]{1,0:T(8,128)} %get-tuple-element.65.refs_0_, ...), custom_call_target="tpu_custom_call" | custom-call | tf_op jit(solution)/shard_map/finish_all/pallas_call | solution.py:1187
  190.1 0.0 copy-done
  190.1 1.0 copy.32
Async XLA Ops:
  182.6 7.5 %copy-start = (bf16[768,768]{1,0:T(8,128)(2,1)S(1)}, bf16[768,768]{1,0:T(8,128)(2,1)}, u32[]{:S(2)}) copy-start(bf16[768,768]{1,0:T(8,128)(2,1)} %get-tuple-element.50) | copy-start | bytes 3538948
